TPU v7x, 256 devices: a whole 4x4x8 slice. The times are simulated.
256 devices in a mesh: clus: 16 (over z, core), node: 16 (over x, y).
Axes of the slice: x: 4, y: 4, z: 8, core: 2. Of those that a mesh axis runs over, the one named last changes fastest.
Arguments:
- node_feats: bfloat16 [16, 2048, 1024], P('clus', 'node'), may hold values from -6 to 6
- cotangent: bfloat16 [16, 2048, 1024], P('clus', 'node'), may hold values from -6 to 6
- w_query: bfloat16 [1024, 1024], replicated, may hold values from -0.1875 to 0.1875
- w_key: bfloat16 [1024, 1024], replicated, may hold values from -0.1875 to 0.1875
- w_value: bfloat16 [1024, 1024], replicated, may hold values from -0.1875 to 0.1875
- w_out: bfloat16 [1024, 1024], replicated, may hold values from -0.1875 to 0.1875
- eigvec: bfloat16 [16, 64, 2048], P('clus'), may hold values from -3.5 to 3.5
- eig_weight: float32 [16, 64], P('node'), may hold values from 0.1 to 1
- block_mask: int32 [16, 16, 16, 16], P('clus', 'node'), may hold values from 0 to 1, as said below
Outputs:
- grad_nodes: bfloat16 [16, 2048, 1024], P('clus', 'node')
- grad_eigvec: float32 [16, 64, 2048], P('clus', None, 'node')
- grad_weight: float32 [16, 64], P('node')
- grad_proj: float32 [4, 1024, 1024], P(None, 'clus', 'node')
Inputs may be any that keep to these rules, and one draw needn't show every extreme that they name: `block_mask`: each entry is 0 or 1; every diagonal tile is 1; the share of present tiles differs between clusters and heads.
All inputs are finite; a program needn't handle non-finite values.
Results may differ from a plain program's by a relative error of at most 0.012.
The roundings to bfloat16 on the way count: a program that leaves them out, or rounds other values in their place, can miss the bound.
Values may be sent and summed in bfloat16 or wider, within the bound.
A program may use at most 128 MiB of HBM per device.

v0:
```python
import jax
import jax.numpy as jnp
from jax import lax
from jax.sharding import PartitionSpec as P


def body(node_feats, cotangent, w_query, w_key, w_value, w_out, eigvec, eig_weight, block_mask):
    node_rows = node_feats[0]
    grads_in = cotangent[0]
    query = jnp.dot(node_rows, w_query, preferred_element_type=jnp.float32).astype(jnp.bfloat16)
    keys_local = jnp.dot(node_rows, w_key, preferred_element_type=jnp.float32).astype(jnp.bfloat16)
    values_local = jnp.dot(node_rows, w_value, preferred_element_type=jnp.float32).astype(
        jnp.bfloat16
    )
    d_att = jnp.dot(grads_in, w_out, preferred_element_type=jnp.float32).astype(jnp.bfloat16)
    head_data = lax.all_to_all(
        jnp.stack([query, keys_local, values_local, d_att]),
        "node",
        split_axis=2,
        concat_axis=1,
        tiled=True,
    )
    node_count = head_data.shape[1]
    head_width = head_data.shape[2]
    heads_dev = eig_weight.shape[0]
    head_size = head_width // heads_dev
    by_head = head_data.reshape(4, node_count, heads_dev, head_size)
    query_heads = by_head[0]
    keys_heads = by_head[1]
    values_heads = by_head[2]
    dout_heads = by_head[3]
    eig_all = eigvec[0]
    eig_float = eig_all.astype(jnp.float32)
    weighted = (eig_weight[:, :, None] * eig_float[None]).astype(jnp.bfloat16)
    tile_mask = block_mask[0]
    tile_count = tile_mask.shape[2]
    tile_size = node_count // tile_count
    block_rows = min(512, node_count)
    block_count = node_count // block_rows
    score_scale = head_size ** (-0.5)

    def one_block(totals, block_index):
        key_grad, value_grad, eig_right, weight_grad = totals
        offset = block_index * block_rows
        query_block = lax.dynamic_slice_in_dim(query_heads, offset, block_rows, 0)
        dout_block = lax.dynamic_slice_in_dim(dout_heads, offset, block_rows, 0)
        eig_block = lax.dynamic_slice_in_dim(eig_all, offset, block_rows, 1)
        eig_bias = jnp.einsum(
            "ki,hkj->hij", eig_block, weighted, preferred_element_type=jnp.float32
        )
        scores = (
            jnp.einsum("ihd,jhd->hij", query_block, keys_heads, preferred_element_type=jnp.float32)
            * score_scale
            + eig_bias
        )
        tile_rows = lax.dynamic_slice_in_dim(
            tile_mask, offset // tile_size, block_rows // tile_size, 1
        )
        present = jnp.broadcast_to(
            tile_rows[:, :, None, :, None] > 0,
            (heads_dev, block_rows // tile_size, tile_size, tile_count, tile_size),
        )
        present = present.reshape(heads_dev, block_rows, node_count)
        masked = jnp.where(present, scores, -jnp.inf)
        row_max = jnp.max(masked, axis=2, keepdims=True)
        raised = jnp.exp(masked - row_max)
        attn_prob = raised / jnp.sum(raised, axis=2, keepdims=True)
        prob_half = attn_prob.astype(jnp.bfloat16)
        out_block = jnp.einsum(
            "hij,jhd->ihd", prob_half, values_heads, preferred_element_type=jnp.float32
        ).astype(jnp.bfloat16)
        dprob = jnp.einsum(
            "ihd,jhd->hij", dout_block, values_heads, preferred_element_type=jnp.float32
        )
        row_delta = jnp.sum(attn_prob * dprob, axis=2, keepdims=True)
        dscore = (attn_prob * (dprob - row_delta)).astype(jnp.bfloat16)
        query_grad = (
            jnp.einsum("hij,jhd->ihd", dscore, keys_heads, preferred_element_type=jnp.float32)
            * score_scale
        ).astype(jnp.bfloat16)
        key_grad = key_grad + jnp.einsum(
            "hij,ihd->jhd", dscore, query_block, preferred_element_type=jnp.float32
        )
        value_grad = value_grad + jnp.einsum(
            "hij,ihd->jhd", prob_half, dout_block, preferred_element_type=jnp.float32
        )
        eig_left = jnp.einsum("hij,kj->hki", dscore, eig_all, preferred_element_type=jnp.float32)
        weight_grad = weight_grad + jnp.sum(eig_left * eig_block.astype(jnp.float32)[None], axis=2)
        eig_right = eig_right + jnp.einsum(
            "hij,ki->hkj", dscore, eig_block, preferred_element_type=jnp.float32
        )
        left_term = jnp.sum(eig_weight[:, :, None] * eig_left, axis=0)
        return ((key_grad, value_grad, eig_right, weight_grad), (out_block, query_grad, left_term))

    initial = (
        jnp.zeros((node_count, heads_dev, head_size), jnp.float32),
        jnp.zeros((node_count, heads_dev, head_size), jnp.float32),
        jnp.zeros((heads_dev, eig_all.shape[0], node_count), jnp.float32),
        jnp.zeros(eig_weight.shape, jnp.float32),
    )
    totals, blocks = lax.scan(one_block, initial, jnp.arange(block_count))
    output_heads = blocks[0].reshape(node_count, head_width)
    query_grad_heads = blocks[1].reshape(node_count, head_width)
    key_grad_heads = (totals[0] * score_scale).astype(jnp.bfloat16).reshape(node_count, head_width)
    value_grad_heads = totals[1].astype(jnp.bfloat16).reshape(node_count, head_width)
    left_all = blocks[2].transpose(1, 0, 2).reshape(eig_all.shape[0], node_count)
    eig_term = left_all + jnp.sum(eig_weight[:, :, None] * totals[2], axis=0)
    returned = lax.all_to_all(
        jnp.stack([output_heads, query_grad_heads, key_grad_heads, value_grad_heads]),
        "node",
        split_axis=1,
        concat_axis=2,
        tiled=True,
    )
    output_nodes = returned[0]
    query_grad_nodes = returned[1]
    key_grad_nodes = returned[2]
    value_grad_nodes = returned[3]
    grad_rows = (
        jnp.einsum("re,de->rd", query_grad_nodes, w_query, preferred_element_type=jnp.float32)
        + jnp.einsum("re,de->rd", key_grad_nodes, w_key, preferred_element_type=jnp.float32)
        + jnp.einsum("re,de->rd", value_grad_nodes, w_value, preferred_element_type=jnp.float32)
    ).astype(jnp.bfloat16)
    grad_eigvec = lax.psum_scatter(eig_term, "node", scatter_dimension=1, tiled=True)
    grad_weight = lax.psum(totals[3], "clus")
    grad_terms = jnp.stack(
        [
            jnp.einsum(
                "rd,re->de", node_rows, query_grad_nodes, preferred_element_type=jnp.float32
            ),
            jnp.einsum("rd,re->de", node_rows, key_grad_nodes, preferred_element_type=jnp.float32),
            jnp.einsum(
                "rd,re->de", node_rows, value_grad_nodes, preferred_element_type=jnp.float32
            ),
            jnp.einsum("rd,re->de", grads_in, output_nodes, preferred_element_type=jnp.float32),
        ]
    )
    col_sums = lax.psum_scatter(grad_terms, "node", scatter_dimension=2, tiled=True)
    grad_proj = lax.psum_scatter(col_sums, "clus", scatter_dimension=1, tiled=True)
    return (grad_rows[None], grad_eigvec[None], grad_weight, grad_proj)


def solution(mesh):
    placed = (
        P("clus", "node", None),
        P("clus", "node", None),
        P(),
        P(),
        P(),
        P(),
        P("clus", None, None),
        P("node", None),
        P("clus", "node", None, None),
    )
    return jax.shard_map(
        body,
        mesh=mesh,
        in_specs=placed,
        out_specs=(
            P("clus", "node", None),
            P("clus", None, "node"),
            P("node", None),
            P(None, "clus", "node"),
        ),
        check_vma=False,
    )
```

profile of v0, /device:TPU:2, one launch (start us, length us, event | category | flops | bytes accessed | tf_op | source)
XLA Modules:
  0.0 431.4 jit_solution(2810686122069880913)
XLA Ops:
  15.3 7.5 %all-to-all-start = ((bf16[4,128,1024]{1,0,2:T(4,128)(2,1)}), bf16[4,128,1024]{1,0,2:T(4,128)(2,1)S(1)}, u32[]{:S(2)}, u32[]{:S(2)}) async-start(bf16[4,128,1024]{1,0,2:T(4,128)(2,1)} %copy.40), calls=%async_computation | async-start | bytes 2097152 | tf_op jit(solution)/shard_map/all_to_all | solution.py:16
  23.7 14.1 %all-to-all-done = bf16[4,128,1024]{1,0,2:T(4,128)(2,1)S(1)} async-done(((bf16[4,128,1024]{1,0,2:T(4,128)(2,1)}), bf16[4,128,1024]{1,0,2:T(4,128)(2,1)S(1)}, u32[]{:S(2)}, u32[]{:S(2)}) %all-to-all-start) | async-done | bytes 1048608 | tf_op jit(solution)/shard_map/all_to_all | solution.py:16
  41.4 74.0 %while.25 = (s32[]{:T(128)}, f32[2048,1,64]{0,2,1:T(8,128)}, f32[2048,1,64]{0,2,1:T(8,128)}, f32[1,64,2048]{2,1,0:T(8,128)}, f32[1,64]{1,0:T(1,128)S(1)}, /*inde...) while((s32[]{:T(128)}, f32[2048,1,64]{0,2,1:T(8,128)}, ...), condition=%wide.region_5.6_spmd.clone, body=%wide.region_0.5_spmd.clone.sunk | while | flops 1224702592 | bytes 83313016 | solution.py:101
  43.7 2.3 broadcast_in_dim.70
  57.3 2.3 fusion.136
  61.9 2.3 broadcast_in_dim.70
  75.6 2.6 fusion.136
  80.5 2.3 broadcast_in_dim.70
  94.2 2.6 fusion.136
  99.1 2.3 broadcast_in_dim.70
  112.8 2.6 fusion.136
  121.1 2.5 copy.48
  123.6 4.4 %reshape.203 = bf16[16,2,16384]{2,1,0:T(2,128)(2,1)S(1)} reshape(bf16[2048,4,64]{2,1,0:T(4,128)(2,1)} %bitcast.283) | data formatting | bytes 2097152
  128.0 19.3 %all_to_all.30 = bf16[16,2,16384]{2,1,0:T(2,128)(2,1)} all-to-all(bf16[16,2,16384]{2,1,0:T(2,128)(2,1)S(1)} %reshape.203), channel_id=1, replica_groups=mesh['clus'=16,'node'=16] {'node'}, dimensions={0} | all-to-all | bytes 2097152 | tf_op jit(solution)/shard_map/all_to_all | solution.py:108
  147.3 5.2 %reshape.204 = bf16[2048,4,64]{2,1,0:T(4,128)(2,1)} reshape(bf16[16,2,16384]{2,1,0:T(2,128)(2,1)} %all_to_all.30) | data formatting | bytes 2097152
  152.6 2.8 copy.56
  158.7 6.0 %pad_maximum_fusion = f32[4,1024,1024]{1,2,0:T(8,128)} fusion(f32[1,1024,1024]{1,2,0:T(8,128)S(1)} %convolution_bitcast_fusion.4, f32[1,1024,1024]{1,2,0:T(8,128)S(1)} %convolution_bitcast_fusion.5, f32[1,1024,1024]{1,2,0:T(8,128)S(1)} %convolution_bitcast_fusion.6, f32[1,1024,1024]{1,2,0:T(8,128)S(1)} %convolution_bitcast_fusion.7), kind=kLoop, calls=%fused_computation.58 | loop fusion | flops 12582912 | bytes 33554432 | tf_op jit(solution)/shard_map/stack | solution.py:126
  164.8 116.6 %reduce-scatter.8.cloned.1.call-done = f32[4,1024,64]{1,2,0:T(8,128)} async-done(((f32[4,1024,1024]{1,2,0:T(8,128)}), f32[4,1024,64]{1,2,0:T(8,128)}) %reduce-scatter.8.cloned.1.call-update) | async-done | bytes 1048592 | tf_op jit(solution)/shard_map/reduce_scatter | solution.py:138
  281.4 2.7 copy.57
  284.1 3.2 reshape.201
  289.4 26.9 %psum.7 = f32[1,64]{1,0:T(1,128)} all-reduce(f32[1,64]{1,0:T(1,128)S(1)} %get-tuple-element.549), channel_id=1, replica_groups=mesh['clus'=16,'node'=16] {'clus'}, use_global_device_ids=true, to_apply=%region_7.8 | all-reduce | flops 64 | bytes 512 | tf_op jit(solution)/shard_map/psum | solution.py:125
  317.2 2.4 convolution_add_fusion.1
  321.2 23.6 %reduce-scatter.10.cloned.1.call-done = f32[64,256]{1,0:T(8,128)} async-done(((f32[1024,256]{1,0:T(8,128)}), f32[64,256]{1,0:T(8,128)}) %reduce-scatter.10.cloned.1.call-update) | async-done | bytes 65552
  346.4 78.4 %reduce-scatter.6.cloned.1.call-done = f32[64,128]{1,0:T(8,128)} async-done(((f32[64,2048]{1,0:T(8,128)}), f32[64,128]{1,0:T(8,128)}) %reduce-scatter.6.cloned.1.call-update) | async-done | bytes 32784 | tf_op jit(solution)/shard_map/reduce_scatter | solution.py:124
  (206 shorter events, 79.1 us)
Async XLA Ops:
  7.2 5.6 %copy-start.9 = (bf16[1,128,1024]{2,1,0:T(8,128)(2,1)S(1)}, bf16[1,128,1024]{2,1,0:T(8,128)(2,1)}, u32[]{:S(2)}) copy-start(bf16[1,128,1024]{2,1,0:T(8,128)(2,1)} %param.11) | copy-start | bytes 786436
  7.2 5.6 %copy-start.13 = (bf16[1024,1024]{1,0:T(8,128)(2,1)S(1)}, bf16[1024,1024]{1,0:T(8,128)(2,1)}, u32[]{:S(2)}) copy-start(bf16[1024,1024]{1,0:T(8,128)(2,1)} %param.15) | copy-start | bytes 6291460
  7.2 6.0 %copy-start.17 = (bf16[1,128,1024]{2,1,0:T(8,128)(2,1)S(1)}, bf16[1,128,1024]{2,1,0:T(8,128)(2,1)}, u32[]{:S(2)}) copy-start(bf16[1,128,1024]{2,1,0:T(8,128)(2,1)} %param.12) | copy-start | bytes 786436
  7.2 6.0 %copy-start.15 = (bf16[1024,1024]{1,0:T(8,128)(2,1)S(1)}, bf16[1024,1024]{1,0:T(8,128)(2,1)}, u32[]{:S(2)}) copy-start(bf16[1024,1024]{1,0:T(8,128)(2,1)} %param.16) | copy-start | bytes 6291460
  13.2 9.7 %copy-start.2 = (bf16[1,64,2048]{2,1,0:T(8,128)(2,1)S(1)}, bf16[1,64,2048]{2,1,0:T(8,128)(2,1)}, u32[]{:S(2)}) copy-start(bf16[1,64,2048]{2,1,0:T(8,128)(2,1)} %param.17) | copy-start | bytes 786436
  13.2 9.7 %copy-start.19 = (f32[1,64]{1,0:T(1,128)S(1)}, f32[1,64]{1,0:T(1,128)}, u32[]{:S(2)}) copy-start(f32[1,64]{1,0:T(1,128)} %param.18) | copy-start | bytes 772
  15.3 22.5 %all-to-all-start = ((bf16[4,128,1024]{1,0,2:T(4,128)(2,1)}), bf16[4,128,1024]{1,0,2:T(4,128)(2,1)S(1)}, u32[]{:S(2)}, u32[]{:S(2)}) async-start(bf16[4,128,1024]{1,0,2:T(4,128)(2,1)} %copy.40), calls=%async_computation | async-start | bytes 2097152 | tf_op jit(solution)/shard_map/all_to_all | solution.py:16
  22.8 258.6 %reduce-scatter.8.cloned.1.call-start = ((), (), s32[]{:S(2)}) async-start(), calls=%async_computation.6 | async-start | bytes 17825792 | tf_op jit(solution)/shard_map/reduce_scatter | solution.py:138
  51.7 3.7 copy-start.4
  55.9 3.7 copy-start.5
  69.9 3.7 copy-start.4
  72.2 2.8 copy-start.6
  74.2 4.1 copy-start.5
  88.5 3.7 copy-start.4
  90.8 2.8 copy-start.6
  92.8 4.0 copy-start.5
  107.1 3.7 copy-start.4
  109.4 2.8 copy-start.6
  111.4 4.0 copy-start.5
  152.6 3.3 copy-start.10
  164.7 123.8 %copy-start.8 = (f32[1,64,2048]{2,1,0:T(8,128)S(1)}, f32[1,64,2048]{2,1,0:T(8,128)}, u32[]{:S(2)}) copy-start(f32[1,64,2048]{2,1,0:T(8,128)} %get-tuple-element.548) | copy-start | bytes 1572868
  164.7 180.1 %reduce-scatter.10.cloned.1.call-start = ((), (), s32[]{:S(2)}) async-start(), calls=%async_computation.7 | async-start | bytes 1114112
  287.4 137.5 %reduce-scatter.6.cloned.1.call-start = ((), (), s32[]{:S(2)}) async-start(), calls=%async_computation.5 | async-start | bytes 557056 | tf_op jit(solution)/shard_map/reduce_scatter | solution.py:124
  316.4 3.3 copy-start.14
  (27 other events, 44.3 us)
Sparse Core Ops, SparseCore 0:
  164.8 116.5 reduce-scatter.7
  287.5 57.2 reduce-scatter.9
  349.3 75.5 reduce-scatter.5
where the time goes:
time: 433 us; the launch traced here: 431 us
  waiting for transfers between devices  233 us (54%)
  matrix products  58.3 us (13%)
  local copies, waits for them, and re-layouts  48.1 us (11%)
  blocking collectives  46.2 us (11%)
  other arithmetic  21.1 us (5%)
  between operations  14.2 us (3%)
  starting transfers between devices  7.6 us (2%)
    reduce_scatter x1, waiting for transfers between devices, body(): lax.psum_scatter(grad_terms, 'node', scatter_dimension=2, tiled=True)  117 us
    reduce_scatter x1, waiting for transfers between devices, body(): lax.psum_scatter(eig_term, 'node', scatter_dimension=1, tiled=True)  78.4 us
    psum x1, blocking collectives, body(): grad_weight = lax.psum(totals[3], 'clus')  26.9 us
    unnamed x4, waiting for transfers between devices  23.7 us
    all_to_all x1, blocking collectives, body(): lax.all_to_all(jnp.stack([output_heads, query_grad_heads, key_grad_heads,...  19.3 us
    unnamed x28, local copies, waits for them, and re-layouts  18.8 us
    all_to_all x1, waiting for transfers between devices, body(): lax.all_to_all(jnp.stack([query, keys_local, values_local, d_att]), 'node...  14.1 us
    broadcast_in_dim x8, local copies, waits for them, and re-layouts, one_block(): jnp.broadcast_to(tile_rows[:, :, None, :, None] > 0, (heads_dev, block_ro...  10.5 us
  transfers between devices with their start and end apart: 4, of which 4 were waited for; matrix products, arithmetic and copies ran while one was open for 2% of the time, Pallas kernels for 0%

commit v1 on v0

--- a/solution.py
+++ b/solution.py
@@ -105,12 +105,20 @@
     value_grad_heads = totals[1].astype(jnp.bfloat16).reshape(node_count, head_width)
     left_all = blocks[2].transpose(1, 0, 2).reshape(eig_all.shape[0], node_count)
     eig_term = left_all + jnp.sum(eig_weight[:, :, None] * totals[2], axis=0)
-    returned = lax.all_to_all(
-        jnp.stack([output_heads, query_grad_heads, key_grad_heads, value_grad_heads]),
-        "node",
-        split_axis=1,
-        concat_axis=2,
-        tiled=True,
+    returned = jnp.concatenate(
+        lax.all_to_all(
+            jnp.stack(
+                jnp.split(
+                    jnp.stack([output_heads, query_grad_heads, key_grad_heads, value_grad_heads]),
+                    lax.axis_size("node"),
+                    axis=1,
+                )
+            ),
+            "node",
+            0,
+            0,
+        ),
+        axis=2,
     )
     output_nodes = returned[0]
     query_grad_nodes = returned[1]

time: 433 us -> 416 us (0.961)
  local copies, waits for them, and re-layouts: 48.1 us -> 32.6 us
    unnamed x28 -> x41, local copies, waits for them, and re-layouts: 18.8 us -> 9.58 us
where the time goes in v1:
time: 416 us; the launch traced here: 415 us
  waiting for transfers between devices  233 us (56%)
  matrix products  58.3 us (14%)
  blocking collectives  46.1 us (11%)
  local copies, waits for them, and re-layouts  32.6 us (8%)
  other arithmetic  20.1 us (5%)
  between operations  14.2 us (3%)
  starting transfers between devices  7.6 us (2%)
    reduce_scatter x1, waiting for transfers between devices, body(): lax.psum_scatter(grad_terms, 'node', scatter_dimension=2, tiled=True)  117 us
    reduce_scatter x1, waiting for transfers between devices, body(): lax.psum_scatter(eig_term, 'node', scatter_dimension=1, tiled=True)  78.6 us
    psum x1, blocking collectives, body(): grad_weight = lax.psum(totals[3], 'clus')  26.9 us
    unnamed x4, waiting for transfers between devices  23.6 us
    all_to_all x1, blocking collectives, body(): lax.all_to_all(jnp.stack(jnp.split(jnp.stack([output_heads, query_grad_he...  19.2 us
    all_to_all x1, waiting for transfers between devices, body(): lax.all_to_all(jnp.stack([query, keys_local, values_local, d_att]), 'node...  14.1 us
    broadcast_in_dim x8, local copies, waits for them, and re-layouts, one_block(): jnp.broadcast_to(tile_rows[:, :, None, :, None] > 0, (heads_dev, block_ro...  10.5 us
    dot_general x4, matrix products, one_block(): jnp.einsum('hij,ihd->jhd', dscore, query_block, preferred_element_type=jn...  10.1 us
  transfers between devices with their start and end apart: 4, of which 4 were waited for; matrix products, arithmetic and copies ran while one was open for 2% of the time, Pallas kernels for 0%

profile of v1, /device:TPU:2, one launch (start us, length us, event | category | flops | bytes accessed | tf_op | source)
XLA Modules:
  0.0 414.9 jit_solution(9513065504960201619)
XLA Ops:
  8.8 1.8 fusion.53
  10.6 2.1 fusion.54
  15.3 7.5 %all-to-all-start = ((bf16[4,128,1024]{1,0,2:T(4,128)(2,1)}), bf16[4,128,1024]{1,0,2:T(4,128)(2,1)S(1)}, u32[]{:S(2)}, u32[]{:S(2)}) async-start(bf16[4,128,1024]{1,0,2:T(4,128)(2,1)} %copy.28), calls=%async_computation | async-start | bytes 2097152 | tf_op jit(solution)/shard_map/all_to_all | solution.py:16
  23.7 14.1 %all-to-all-done = bf16[4,128,1024]{1,0,2:T(4,128)(2,1)S(1)} async-done(((bf16[4,128,1024]{1,0,2:T(4,128)(2,1)}), bf16[4,128,1024]{1,0,2:T(4,128)(2,1)S(1)}, u32[]{:S(2)}, u32[]{:S(2)}) %all-to-all-start) | async-done | bytes 1048608 | tf_op jit(solution)/shard_map/all_to_all | solution.py:16
  41.4 74.0 %while.25 = (s32[]{:T(128)}, f32[2048,1,64]{0,2,1:T(8,128)}, f32[2048,1,64]{0,2,1:T(8,128)}, f32[1,64,2048]{2,1,0:T(8,128)}, f32[1,64]{1,0:T(1,128)S(1)}, /*inde...) while((s32[]{:T(128)}, f32[2048,1,64]{0,2,1:T(8,128)}, ...), condition=%wide.region_5.6_spmd.clone, body=%wide.region_0.5_spmd.clone.sunk | while | flops 1224702592 | bytes 83313016 | solution.py:101
  43.7 2.3 broadcast_in_dim.70
  57.3 2.3 fusion.152
  61.9 2.3 broadcast_in_dim.70
  75.6 2.6 fusion.152
  80.5 2.3 broadcast_in_dim.70
  82.8 1.7 fusion.147
  94.2 2.6 fusion.152
  99.1 2.3 broadcast_in_dim.70
  101.4 1.7 fusion.147
  112.8 2.6 fusion.152
  120.0 19.2 %all_to_all.20 = bf16[16,4,128,64]{2,3,1,0:T(8,128)(2,1)S(1)} all-to-all(bf16[16,4,128,64]{2,3,1,0:T(8,128)(2,1)S(1)} %fusion.66), channel_id=1, replica_groups=mesh['clus'=16,'node'=16] {'node'}, dimensions={0} | all-to-all | bytes 2097152 | tf_op jit(solution)/shard_map/all_to_all | solution.py:109
  142.1 6.0 %pad_maximum_fusion = f32[4,1024,1024]{1,2,0:T(8,128)} fusion(f32[1,1024,1024]{1,2,0:T(8,128)S(1)} %convolution_bitcast_fusion.4, f32[1,1024,1024]{1,2,0:T(8,128)S(1)} %convolution_bitcast_fusion.5, f32[1,1024,1024]{1,2,0:T(8,128)S(1)} %convolution_bitcast_fusion.6, f32[1,1024,1024]{1,2,0:T(8,128)S(1)} %convolution_bitcast_fusion.7), kind=kLoop, calls=%fused_computation.58 | loop fusion | flops 12582912 | bytes 33554432 | tf_op jit(solution)/shard_map/stack | solution.py:134
  148.2 116.6 %reduce-scatter.8.cloned.1.call-done = f32[4,1024,64]{1,2,0:T(8,128)} async-done(((f32[4,1024,1024]{1,2,0:T(8,128)}), f32[4,1024,64]{1,2,0:T(8,128)}) %reduce-scatter.8.cloned.1.call-update) | async-done | bytes 1048592 | tf_op jit(solution)/shard_map/reduce_scatter | solution.py:146
  264.9 2.7 copy.38
  267.6 3.2 reshape.206
  272.9 26.9 %psum.7 = f32[1,64]{1,0:T(1,128)} all-reduce(f32[1,64]{1,0:T(1,128)S(1)} %get-tuple-element.545), channel_id=1, replica_groups=mesh['clus'=16,'node'=16] {'clus'}, use_global_device_ids=true, to_apply=%region_7.8 | all-reduce | flops 64 | bytes 512 | tf_op jit(solution)/shard_map/psum | solution.py:133
  300.6 2.4 convolution_add_fusion.1
  304.6 23.5 %reduce-scatter.10.cloned.1.call-done = f32[64,256]{1,0:T(8,128)} async-done(((f32[1024,256]{1,0:T(8,128)}), f32[64,256]{1,0:T(8,128)}) %reduce-scatter.10.cloned.1.call-update) | async-done | bytes 65552
  329.8 78.6 %reduce-scatter.6.cloned.1.call-done = f32[64,128]{1,0:T(8,128)} async-done(((f32[64,2048]{1,0:T(8,128)}), f32[64,128]{1,0:T(8,128)}) %reduce-scatter.6.cloned.1.call-update) | async-done | bytes 32784 | tf_op jit(solution)/shard_map/reduce_scatter | solution.py:132
  (214 shorter events, 70.2 us)
Async XLA Ops:
  7.2 5.6 %copy-start.9 = (bf16[1,128,1024]{2,1,0:T(8,128)(2,1)S(1)}, bf16[1,128,1024]{2,1,0:T(8,128)(2,1)}, u32[]{:S(2)}) copy-start(bf16[1,128,1024]{2,1,0:T(8,128)(2,1)} %param.11) | copy-start | bytes 786436
  7.2 5.6 %copy-start.13 = (bf16[1024,1024]{1,0:T(8,128)(2,1)S(1)}, bf16[1024,1024]{1,0:T(8,128)(2,1)}, u32[]{:S(2)}) copy-start(bf16[1024,1024]{1,0:T(8,128)(2,1)} %param.15) | copy-start | bytes 6291460
  7.2 6.0 %copy-start.17 = (bf16[1,128,1024]{2,1,0:T(8,128)(2,1)S(1)}, bf16[1,128,1024]{2,1,0:T(8,128)(2,1)}, u32[]{:S(2)}) copy-start(bf16[1,128,1024]{2,1,0:T(8,128)(2,1)} %param.12) | copy-start | bytes 786436
  7.2 6.0 %copy-start.15 = (bf16[1024,1024]{1,0:T(8,128)(2,1)S(1)}, bf16[1024,1024]{1,0:T(8,128)(2,1)}, u32[]{:S(2)}) copy-start(bf16[1024,1024]{1,0:T(8,128)(2,1)} %param.16) | copy-start | bytes 6291460
  13.2 9.7 %copy-start.2 = (bf16[1,64,2048]{2,1,0:T(8,128)(2,1)S(1)}, bf16[1,64,2048]{2,1,0:T(8,128)(2,1)}, u32[]{:S(2)}) copy-start(bf16[1,64,2048]{2,1,0:T(8,128)(2,1)} %param.17) | copy-start | bytes 786436
  13.2 9.7 %copy-start.19 = (f32[1,64]{1,0:T(1,128)S(1)}, f32[1,64]{1,0:T(1,128)}, u32[]{:S(2)}) copy-start(f32[1,64]{1,0:T(1,128)} %param.18) | copy-start | bytes 772
  15.3 22.5 %all-to-all-start = ((bf16[4,128,1024]{1,0,2:T(4,128)(2,1)}), bf16[4,128,1024]{1,0,2:T(4,128)(2,1)S(1)}, u32[]{:S(2)}, u32[]{:S(2)}) async-start(bf16[4,128,1024]{1,0,2:T(4,128)(2,1)} %copy.28), calls=%async_computation | async-start | bytes 2097152 | tf_op jit(solution)/shard_map/all_to_all | solution.py:16
  22.8 242.1 %reduce-scatter.8.cloned.1.call-start = ((), (), s32[]{:S(2)}) async-start(), calls=%async_computation.6 | async-start | bytes 17825792 | tf_op jit(solution)/shard_map/reduce_scatter | solution.py:146
  51.7 3.7 copy-start.4
  55.9 3.7 copy-start.5
  69.9 3.7 copy-start.4
  72.2 2.8 copy-start.6
  74.2 4.1 copy-start.5
  88.5 3.7 copy-start.4
  90.8 2.8 copy-start.6
  92.8 4.0 copy-start.5
  107.1 3.7 copy-start.4
  109.4 2.8 copy-start.6
  111.4 4.0 copy-start.5
  119.3 20.0 %copy-start.10 = (bf16[1,128,1024]{2,1,0:T(8,128)(2,1)S(1)}, bf16[1,128,1024]{2,1,0:T(8,128)(2,1)}, u32[]{:S(2)}) copy-start(bf16[1,128,1024]{2,1,0:T(8,128)(2,1)} %param.11) | copy-start | bytes 786436
  148.2 123.8 %copy-start.8 = (f32[1,64,2048]{2,1,0:T(8,128)S(1)}, f32[1,64,2048]{2,1,0:T(8,128)}, u32[]{:S(2)}) copy-start(f32[1,64,2048]{2,1,0:T(8,128)} %get-tuple-element.544) | copy-start | bytes 1572868
  148.2 180.0 %reduce-scatter.10.cloned.1.call-start = ((), (), s32[]{:S(2)}) async-start(), calls=%async_computation.7 | async-start | bytes 1114112
  270.9 137.5 %reduce-scatter.6.cloned.1.call-start = ((), (), s32[]{:S(2)}) async-start(), calls=%async_computation.5 | async-start | bytes 557056 | tf_op jit(solution)/shard_map/reduce_scatter | solution.py:132
  299.8 3.3 copy-start.14
  (27 other events, 44.3 us)
Sparse Core Ops, SparseCore 0:
  148.3 116.5 reduce-scatter.7
  271.0 57.1 reduce-scatter.9
  332.6 75.7 reduce-scatter.5
